TPU v7x, 32 devices: a whole 2x2x4 slice. The times are simulated.
32 devices in a mesh: grp: 2 (over x), tile: 16 (over z, y, core).
Axes of the slice: x: 2, y: 2, z: 4, core: 2. Of those that a mesh axis runs over, the one named last changes fastest.
Arguments:
- full_resolution_frames: bfloat16 [32, 2, 512, 512], P(('grp', 'tile')), parts along dimension 0, may hold values from -24 to 24
- height_angle_factor: float32 [1024, 512], P('grp'), parts along dimension 0, may hold values from -4 to 4
- normal_spacings: float32 [32], P('grp'), parts along dimension 0, may hold values from -2 to 2
- couple_entry_flags: int32 [16, 3], replicated, may hold values from 0 to 1, as said below
- block_target_indices: int32 [32, 64], P('grp'), parts along dimension 0, may hold values from 0 to 255, as said below
- block_target_totals: int32 [32], P('grp'), parts along dimension 0, may hold values from 1 to 64, as said below
Outputs:
- coherence: float32 [32, 3, 128, 32], P(('grp', 'tile')), parts along dimension 0
- velocities: float32 [2048, 15], P(('grp', 'tile')), parts along dimension 0
There are 2 independent parts, one for each index of `grp`. A program takes and returns all parts, laid end to end along the dimension named above; an argument that names none is the same for every part. Nothing has to cross between parts.
Inputs may be any that keep to these rules, and one draw needn't show every extreme that they name: `couple_entry_flags`: slot k-1 of date d stands for the pair of d and d + k; slot 0 is 1 wherever d + 1 < 16; slots with d + k >= 16 are 0. `block_target_indices`: row t lists distinct looked pixels of tile t; entries at or past the tile's count are 0. `block_target_totals`: some tile has exactly 64.
All inputs are finite; a program needn't handle non-finite values.
Results may differ from a plain program's by a relative error of at most 0.0003.
Values may be sent and summed in bfloat16 or wider, within the bound.
A program may use at most 192 MiB of HBM per device.

v0:
```python
import jax
import jax.numpy as jnp
from jax import lax
from jax.sharding import PartitionSpec as P

LOOK_ROWS = 4
LOOK_COLS = 16
EPSILON = 1e-06


def from_behind(block, axis, distance):
    devices = range(lax.axis_size(axis))
    route = [(i - distance, i) for i in devices if i - distance in devices]
    return lax.ppermute(block, axis, route)


def pooling_matrix(cols):
    column_index = jnp.arange(cols, dtype=jnp.int32)[:, None]
    look_index = jnp.arange(cols // LOOK_COLS, dtype=jnp.int32)[None, :]
    member = (column_index // LOOK_COLS == look_index).astype(jnp.float32)
    return member * (1.0 / (LOOK_ROWS * LOOK_COLS))


def looked(field, pooling):
    rows = field.shape[-2]
    cols = field.shape[-1]
    row_sums = jnp.sum(
        field.reshape(field.shape[:-2] + (rows // LOOK_ROWS, LOOK_ROWS, cols)), axis=-2
    )
    return jnp.einsum("...c,cl->...l", row_sums, pooling, precision=lax.Precision.HIGHEST)


def own_power(own_real, own_imag, pooling):
    return looked(own_real * own_real + own_imag * own_imag, pooling)


def pair_stats(own_real, own_imag, power_own, other_real, other_imag, theta, pooling):
    cross_real = own_real * other_real + own_imag * other_imag
    cross_imag = own_imag * other_real - own_real * other_imag
    cosine = jnp.cos(theta)
    sine = jnp.sin(theta)
    flat_real = cross_real * cosine + cross_imag * sine
    flat_imag = cross_imag * cosine - cross_real * sine
    other_energy = other_real * other_real + other_imag * other_imag
    means = looked(jnp.stack([flat_real, flat_imag, other_energy], axis=0), pooling)
    mean_real = means[0]
    mean_imag = means[1]
    power_other = means[2]
    scale = 1.0 / jnp.sqrt(power_own * power_other + EPSILON)
    return (jnp.sqrt(mean_real * mean_real + mean_imag * mean_imag) * scale, mean_imag * scale)


def inverse_map(couple_entry_flags):
    dates = couple_entry_flags.shape[0]
    later_mates = couple_entry_flags.shape[1]
    count = dates * later_mates
    pair_index = jnp.arange(count, dtype=jnp.int32)
    first_date = pair_index // later_mates
    pair_span = pair_index % later_mates + 1
    interval_index = jnp.arange(dates - 1, dtype=jnp.int32)
    covered = (interval_index[None, :] >= first_date[:, None]) & (
        interval_index[None, :] < (first_date + pair_span)[:, None]
    )
    design = couple_entry_flags.reshape(count).astype(jnp.float32)[:, None] * covered.astype(
        jnp.float32
    )
    normal = jnp.dot(design.T, design, precision=lax.Precision.HIGHEST)
    factor = jnp.linalg.cholesky(normal)
    partial_solve = lax.linalg.triangular_solve(factor, design.T, left_side=True, lower=True)
    return lax.linalg.triangular_solve(
        factor, partial_solve, left_side=True, lower=True, transpose_a=True
    )


def local(
    full_resolution_frames,
    height_angle_factor,
    normal_spacings,
    couple_entry_flags,
    block_target_indices,
    block_target_totals,
):
    tile_count = lax.axis_size("tile")
    entry_location = lax.axis_index("tile")
    dates = couple_entry_flags.shape[0]
    later_mates = couple_entry_flags.shape[1]
    image_rows = height_angle_factor.shape[0]
    image_cols = height_angle_factor.shape[1]
    tile_rows = image_rows // tile_count
    looked_cols = image_cols // LOOK_COLS
    tile_pix = tile_rows // LOOK_ROWS * looked_cols
    slot_count = block_target_indices.shape[1]
    pooling = pooling_matrix(image_cols)
    slots = lax.dynamic_index_in_dim(block_target_indices, entry_location, 0, keepdims=False)
    spacing_extended = jnp.concatenate(
        [normal_spacings, jnp.zeros((later_mates,), normal_spacings.dtype)], axis=0
    )
    own = full_resolution_frames[0].astype(jnp.float32)
    power_own = own_power(own[0], own[1], pooling)
    reference_spacing = lax.dynamic_index_in_dim(normal_spacings, entry_location, 0, keepdims=False)
    cohs = []
    phases = []
    for offset in range(1, later_mates + 1):
        other = from_behind(full_resolution_frames, "tile", -offset)[0].astype(jnp.float32)
        other_base = lax.dynamic_index_in_dim(
            spacing_extended, entry_location + offset, 0, keepdims=False
        )
        theta = (reference_spacing - other_base) * height_angle_factor
        coh, phase = pair_stats(own[0], own[1], power_own, other[0], other[1], theta, pooling)
        cohs.append(coh)
        phases.append(phase)
    coh_stack = jnp.stack(cohs, axis=0)
    phase_stack = jnp.stack(phases, axis=0)
    mask_row = lax.dynamic_slice_in_dim(couple_entry_flags, entry_location, 1, 0).astype(
        jnp.float32
    )
    coherence = coh_stack[None] * mask_row[:, :, None, None]
    phase_local = phase_stack[None]
    arrived = lax.all_to_all(phase_local, "tile", split_axis=2, concat_axis=0, tiled=True)
    phase_tile = arrived.reshape(dates * later_mates, tile_pix)
    picked = jnp.take(phase_tile, slots, axis=1)
    mapping = inverse_map(couple_entry_flags)
    velocities = jnp.dot(picked.T, mapping.T, precision=lax.Precision.HIGHEST)
    own_count = lax.dynamic_index_in_dim(block_target_totals, entry_location, 0, keepdims=False)
    valid = (jnp.arange(slot_count, dtype=jnp.int32) < own_count).astype(jnp.float32)
    return (coherence, velocities * valid[:, None])


def solution(mesh):
    in_specs = (
        P(("grp", "tile"), None, None, None),
        P("grp", None),
        P("grp"),
        P(),
        P("grp", None),
        P("grp"),
    )
    out_specs = (P(("grp", "tile"), None, None, None), P(("grp", "tile"), None))
    return jax.shard_map(local, mesh=mesh, in_specs=in_specs, out_specs=out_specs, check_vma=False)
```

profile of v0, /device:TPU:0, one launch (start us, length us, event | category | flops | bytes accessed | tf_op | source)
XLA Modules:
  0.0 135.5 jit_solution(10515715587612405986)
XLA Ops:
  0.6 1.4 %collective-permute-start = (bf16[1,2,512,512]{3,2,1,0:T(8,128)(2,1)}, bf16[1,2,512,512]{3,2,1,0:T(8,128)(2,1)}, u32[]{:S(2)}, u32[]{:S(2)}) collective-permute-start(bf16[1,2,512,512]{3,2,1,0:T(8,128)(2,1)} %param.6), channel_id=1, source_target_pairs={{1,0},{2,1},{3,2},{4,3},{5,4},{6,5},{7,6},{8,7},{9,8},{10,9},{11,1... | collective-permute-start | bytes 3145736 | tf_op jit(solution)/shard_map/ppermute | solution.py:14
  4.7 1.5 %convert_element_type.38 = f32[1,2,512,512]{3,2,1,0:T(8,128)S(1)} convert(bf16[1,2,512,512]{3,2,1,0:T(8,128)(2,1)} %param.6) | non-fusion elementwise | flops 524288 | bytes 3145728 | tf_op jit(solution)/shard_map/convert_element_type | solution.py:98
  6.8 1.4 %cholesky.16 = f32[15,15]{1,0:T(8,128)S(1)} custom-call(f32[15,15]{1,0:T(8,128)S(1)} %fusion.69), custom_call_target="Cholesky" | custom-call | tf_op jit(solution)/shard_map/jit(cholesky)/cholesky | solution.py:68
  11.1 1.3 compare_convert_fusion
  17.0 1.3 add.193
  19.4 1.9 %reduce_sum.37 = f32[128,512]{1,0:T(8,128)S(1)} reduce(f32[128,4,512]{2,1,0:T(4,128)} %add.193, f32[]{:T(128)} %constant.122.clone.1), dimensions={1}, to_apply=%region_1.2 | reduce | flops 196608 | bytes 1310724 | tf_op jit(solution)/shard_map/reduce_sum | solution.py:27
  21.7 1.5 %convert_element_type.39 = f32[1,2,512,512]{3,2,1,0:T(8,128)S(1)} convert(bf16[1,2,512,512]{3,2,1,0:T(8,128)(2,1)} %collective-permute-done) | non-fusion elementwise | flops 524288 | bytes 3145728 | tf_op jit(solution)/shard_map/convert_element_type | solution.py:104
  23.2 1.3 copy-done
  26.1 5.7 %collective-permute-done.2 = bf16[1,2,512,512]{3,2,1,0:T(8,128)(2,1)} collective-permute-done((bf16[1,2,512,512]{3,2,1,0:T(8,128)(2,1)}, bf16[1,2,512,512]{3,2,1,0:T(8,128)(2,1)}, u32[]{:S(2)}, u32[]{:S(2)}) %collective-permute-start.2) | collective-permute-done | bytes 1048608 | tf_op jit(solution)/shard_map/ppermute | solution.py:14
  31.8 1.5 %convert_element_type.41 = f32[1,2,512,512]{3,2,1,0:T(8,128)S(1)} convert(bf16[1,2,512,512]{3,2,1,0:T(8,128)(2,1)} %collective-permute-done.2) | non-fusion elementwise | flops 524288 | bytes 3145728 | tf_op jit(solution)/shard_map/convert_element_type | solution.py:104
  34.5 16.1 %collective-permute-done.1 = bf16[1,2,512,512]{3,2,1,0:T(8,128)(2,1)} collective-permute-done((bf16[1,2,512,512]{3,2,1,0:T(8,128)(2,1)}, bf16[1,2,512,512]{3,2,1,0:T(8,128)(2,1)}, u32[]{:S(2)}, u32[]{:S(2)}) %collective-permute-start.1) | collective-permute-done | bytes 1048608 | tf_op jit(solution)/shard_map/ppermute | solution.py:14
  50.6 1.5 %convert_element_type.40 = f32[1,2,512,512]{3,2,1,0:T(8,128)S(1)} convert(bf16[1,2,512,512]{3,2,1,0:T(8,128)(2,1)} %collective-permute-done.1) | non-fusion elementwise | flops 524288 | bytes 3145728 | tf_op jit(solution)/shard_map/convert_element_type | solution.py:104
  52.4 1.3 copy-done.1
  54.0 13.0 %fusion.4 = (f32[512,512]{1,0:T(8,128)}, f32[1,1,512,512]{3,2,1,0:T(8,128)S(1)}, f32[1,1,512,512]{3,2,1,0:T(8,128)S(1)}, f32[512,512]{1,0:T(8,128)}, f32[1,1,512...) fusion(f32[512,512]{1,0:T(8,128)S(1)} %copy-done.10, ...), kind=kLoop, calls=%fused_computation.19 | loop fusion | flops 7864320 | bytes 18874380 | tf_op jit(solution)/shard_map/add | solution.py:42
  67.0 12.5 %fusion.5 = (f32[512,512]{1,0:T(8,128)}, f32[512,512]{1,0:T(8,128)}, f32[512,512]{1,0:T(8,128)}) fusion(f32[1,1,512,512]{3,2,1,0:T(8,128)S(1)} %get-tuple-element.4, f32[1,1,512,512]{3,2,1,0:T(8,128)S(1)} %get-tuple-element.3, f32[512,512]{1,0:T(8,128)S(1)} %copy-done.10, f32[]{:T(128)} %bitcast.1, f32[1,1,512,512]{3,2,1,0:T(8,128)S(1)} %get-tuple-element.16, ...), kind=kLoop, calls=%fused_computation.20 | loop fusion | flops 3145728 | bytes 10485772 | tf_op jit(solution)/shard_map/sub | solution.py:43
  79.5 2.7 %stack.61 = f32[1,128,4,512]{3,2,1,0:T(4,128)} reshape(f32[512,512]{1,0:T(8,128)} %get-tuple-element.17) | data formatting | bytes 2097152 | tf_op jit(solution)/shard_map/stack | solution.py:45
  84.8 2.7 %stack.71 = f32[1,128,4,512]{3,2,1,0:T(4,128)} reshape(f32[512,512]{1,0:T(8,128)} %get-tuple-element.19) | data formatting | bytes 2097152 | tf_op jit(solution)/shard_map/stack | solution.py:45
  88.8 3.9 %maximum_reduce_fusion = f32[3,128,512]{2,1,0:T(8,128)S(1)} fusion(f32[1,128,4,512]{3,2,1,0:T(4,128)S(1)} %copy-done.6, f32[1,128,4,512]{3,2,1,0:T(4,128)} %stack.61, f32[1,128,4,512]{3,2,1,0:T(4,128)} %stack.60), kind=kLoop, calls=%fused_computation.1 | loop fusion | flops 2162688 | bytes 3932160 | tf_op jit(solution)/shard_map/reduce_sum | solution.py:27
  93.6 2.2 %maximum_reduce_fusion.2 = f32[3,128,512]{2,1,0:T(8,128)S(1)} fusion(f32[1,128,4,512]{3,2,1,0:T(4,128)S(1)} %copy-done.7, f32[1,128,4,512]{3,2,1,0:T(4,128)S(1)} %copy-done.8, f32[1,128,4,512]{3,2,1,0:T(4,128)S(1)} %copy-done.9), kind=kLoop, calls=%fused_computation.3 | loop fusion | flops 2162688 | bytes 3932160 | tf_op jit(solution)/shard_map/reduce_sum | solution.py:27
  96.9 1.5 %stack.66 = f32[1,128,4,512]{3,2,1,0:T(4,128)S(1)} reshape(f32[512,512]{1,0:T(8,128)} %get-tuple-element.18) | data formatting | bytes 2097152 | tf_op jit(solution)/shard_map/stack | solution.py:45
  98.5 1.3 stack.65
  99.8 3.4 %maximum_reduce_fusion.1 = f32[3,128,512]{2,1,0:T(8,128)S(1)} fusion(f32[1,128,4,512]{3,2,1,0:T(4,128)S(1)} %stack.67, f32[1,128,4,512]{3,2,1,0:T(4,128)S(1)} %stack.66, f32[1,128,4,512]{3,2,1,0:T(4,128)} %stack.65), kind=kLoop, calls=%fused_computation.2 | loop fusion | flops 2162688 | bytes 3932160 | tf_op jit(solution)/shard_map/reduce_sum | solution.py:27
  107.1 18.8 %all-to-all-start = ((f32[16,1,768]{2,1,0:T(1,128)}), f32[16,1,768]{2,1,0:T(1,128)S(1)}, u32[]{:S(2)}, u32[]{:S(2)}) async-start(f32[16,1,768]{2,1,0:T(1,128)} %reshape.283), calls=%async_computation | async-start | bytes 98304 | tf_op jit(solution)/shard_map/all_to_all | solution.py:119
  126.6 6.1 %all-to-all-done = f32[16,1,768]{2,1,0:T(1,128)S(1)} async-done(((f32[16,1,768]{2,1,0:T(1,128)}), f32[16,1,768]{2,1,0:T(1,128)S(1)}, u32[]{:S(2)}, u32[]{:S(2)}) %all-to-all-start) | async-done | bytes 49184 | tf_op jit(solution)/shard_map/all_to_all | solution.py:119
  (75 shorter events, 24.8 us)
Async XLA Ops:
  0.6 5.6 %copy-start.11 = (s32[16,3]{0,1:T(4,128)S(1)}, s32[16,3]{0,1:T(4,128)}, u32[]{:S(2)}) copy-start(s32[16,3]{0,1:T(4,128)} %param.9) | copy-start | bytes 580
  0.6 8.9 %copy-start.13 = (s32[16]{0:T(128)S(1)}, s32[16]{0:T(128)}, u32[]{:S(2)}) copy-start(s32[16]{0:T(128)} %param.11) | copy-start | bytes 196
  0.6 21.0 %collective-permute-start = (bf16[1,2,512,512]{3,2,1,0:T(8,128)(2,1)}, bf16[1,2,512,512]{3,2,1,0:T(8,128)(2,1)}, u32[]{:S(2)}, u32[]{:S(2)}) collective-permute-start(bf16[1,2,512,512]{3,2,1,0:T(8,128)(2,1)} %param.6), channel_id=1, source_target_pairs={{1,0},{2,1},{3,2},{4,3},{5,4},{6,5},{7,6},{8,7},{9,8},{10,9},{11,1... | collective-permute-start | bytes 3145736 | tf_op jit(solution)/shard_map/ppermute | solution.py:14
  2.1 29.7 %collective-permute-start.2 = (bf16[1,2,512,512]{3,2,1,0:T(8,128)(2,1)}, bf16[1,2,512,512]{3,2,1,0:T(8,128)(2,1)}, u32[]{:S(2)}, u32[]{:S(2)}) collective-permute-start(bf16[1,2,512,512]{3,2,1,0:T(8,128)(2,1)} %param.6), channel_id=1, source_target_pairs={{3,0},{4,1},{5,2},{6,3},{7,4},{8,5},{9,6},{10,7},{11,8},{12,9},{13... | collective-permute-start | bytes 3145736 | tf_op jit(solution)/shard_map/ppermute | solution.py:14
  3.4 47.3 %collective-permute-start.1 = (bf16[1,2,512,512]{3,2,1,0:T(8,128)(2,1)}, bf16[1,2,512,512]{3,2,1,0:T(8,128)(2,1)}, u32[]{:S(2)}, u32[]{:S(2)}) collective-permute-start(bf16[1,2,512,512]{3,2,1,0:T(8,128)(2,1)} %param.6), channel_id=1, source_target_pairs={{2,0},{3,1},{4,2},{5,3},{6,4},{7,5},{8,6},{9,7},{10,8},{11,9},{12,... | collective-permute-start | bytes 3145736 | tf_op jit(solution)/shard_map/ppermute | solution.py:14
  6.2 6.4 %copy-start.12 = (f32[16]{0:T(128)S(1)}, f32[16]{0:T(128)}, u32[]{:S(2)}) copy-start(f32[16]{0:T(128)} %param.8) | copy-start | bytes 196
  23.2 1.4 %copy-start = (f32[1,2,512,512]{3,2,1,0:T(8,128)}, f32[1,2,512,512]{3,2,1,0:T(8,128)S(1)}, u32[]{:S(2)}) copy-start(f32[1,2,512,512]{3,2,1,0:T(8,128)S(1)} %convert_element_type.39) | copy-start | bytes 6291460
  52.2 1.6 %copy-start.1 = (f32[1,2,512,512]{3,2,1,0:T(8,128)S(1)}, f32[1,2,512,512]{3,2,1,0:T(8,128)}, u32[]{:S(2)}) copy-start(f32[1,2,512,512]{3,2,1,0:T(8,128)} %copy-done) | copy-start | bytes 6291460
  52.2 1.9 %copy-start.10 = (f32[512,512]{1,0:T(8,128)S(1)}, f32[512,512]{1,0:T(8,128)}, u32[]{:S(2)}) copy-start(f32[512,512]{1,0:T(8,128)} %param.7) | copy-start | bytes 3145732
  79.5 2.7 %copy-start.5 = (f32[512,512]{1,0:T(8,128)S(1)}, f32[512,512]{1,0:T(8,128)}, u32[]{:S(2)}) copy-start(f32[512,512]{1,0:T(8,128)} %get-tuple-element.2) | copy-start | bytes 3145732
  79.5 4.0 %copy-start.3 = (f32[1,1,512,512]{3,2,1,0:T(8,128)S(1)}, f32[1,1,512,512]{3,2,1,0:T(8,128)}, u32[]{:S(2)}) copy-start(f32[1,1,512,512]{3,2,1,0:T(8,128)} %multiply_add_fusion) | copy-start | bytes 3145732
  83.5 4.0 %copy-start.4 = (f32[512,512]{1,0:T(8,128)S(1)}, f32[512,512]{1,0:T(8,128)}, u32[]{:S(2)}) copy-start(f32[512,512]{1,0:T(8,128)} %get-tuple-element.11) | copy-start | bytes 3145732
  84.8 4.0 %copy-start.6 = (f32[1,128,4,512]{3,2,1,0:T(4,128)S(1)}, f32[1,128,4,512]{3,2,1,0:T(4,128)}, u32[]{:S(2)}) copy-start(f32[1,128,4,512]{3,2,1,0:T(4,128)} %stack.62) | copy-start | bytes 3145732
  88.8 4.8 %copy-start.7 = (f32[1,128,4,512]{3,2,1,0:T(4,128)S(1)}, f32[1,128,4,512]{3,2,1,0:T(4,128)}, u32[]{:S(2)}) copy-start(f32[1,128,4,512]{3,2,1,0:T(4,128)} %stack.72) | copy-start | bytes 3145732
  88.8 4.8 %copy-start.8 = (f32[1,128,4,512]{3,2,1,0:T(4,128)S(1)}, f32[1,128,4,512]{3,2,1,0:T(4,128)}, u32[]{:S(2)}) copy-start(f32[1,128,4,512]{3,2,1,0:T(4,128)} %stack.71) | copy-start | bytes 3145732
  88.8 4.8 %copy-start.9 = (f32[1,128,4,512]{3,2,1,0:T(4,128)S(1)}, f32[1,128,4,512]{3,2,1,0:T(4,128)}, u32[]{:S(2)}) copy-start(f32[1,128,4,512]{3,2,1,0:T(4,128)} %stack.70) | copy-start | bytes 3145732
  96.6 1.9 %copy-start.2 = (f32[512,512]{1,0:T(8,128)S(1)}, f32[512,512]{1,0:T(8,128)}, u32[]{:S(2)}) copy-start(f32[512,512]{1,0:T(8,128)} %get-tuple-element.14) | copy-start | bytes 3145732
  107.1 25.6 %all-to-all-start = ((f32[16,1,768]{2,1,0:T(1,128)}), f32[16,1,768]{2,1,0:T(1,128)S(1)}, u32[]{:S(2)}, u32[]{:S(2)}) async-start(f32[16,1,768]{2,1,0:T(1,128)} %reshape.283), calls=%async_computation | async-start | bytes 98304 | tf_op jit(solution)/shard_map/all_to_all | solution.py:119
where the time goes:
time: 136 us; the launch traced here: 135 us
  other arithmetic  53.6 us (39%)
  waiting for transfers between devices  27.9 us (21%)
  starting transfers between devices  22.8 us (17%)
  local copies, waits for them, and re-layouts  22.2 us (16%)
  between operations  4.68 us (3%)
  matrix products  4.33 us (3%)
    ppermute x3, waiting for transfers between devices, from_behind(): return lax.ppermute(block, axis, route)  21.8 us
    all_to_all x1, starting transfers between devices, local(): lax.all_to_all(phase_local, 'tile', split_axis=2, concat_axis=0, tiled=True)  18.8 us
    another operation x9, local copies, waits for them, and re-layouts, pair_stats(): jnp.stack([flat_real, flat_imag, other_energy], axis=0)  13.6 us
    add x1, other arithmetic, pair_stats(): flat_real = cross_real * cosine + cross_imag * sine  13 us
    sub x1, other arithmetic, pair_stats(): flat_imag = cross_imag * cosine - cross_real * sine  12.5 us
    reduce_sum x4, other arithmetic, looked(): jnp.sum(field.reshape(field.shape[:-2] + (rows // LOOK_ROWS, LOOK_ROWS, c...  11.4 us
    all_to_all x1, waiting for transfers between devices, local(): lax.all_to_all(phase_local, 'tile', split_axis=2, concat_axis=0, tiled=True)  6.07 us
    unnamed x31, local copies, waits for them, and re-layouts  4.66 us
  transfers between devices with their start and end apart: 4, of which 3 were waited for; matrix products, arithmetic and copies ran while one was open for 15% of the time, Pallas kernels for 0%

commit v1 on v0

--- a/solution.py
+++ b/solution.py
@@ -116,7 +116,19 @@
     )
     coherence = coh_stack[None] * mask_row[:, :, None, None]
     phase_local = phase_stack[None]
-    arrived = lax.all_to_all(phase_local, "tile", split_axis=2, concat_axis=0, tiled=True)
+    ways, here = (lax.axis_size("tile"), lax.axis_index("tile"))
+    width = phase_local.shape[2] // ways
+    dims = list(phase_local.shape)
+    dims[2] = width
+    height = dims[0]
+    dims[0] = height * ways
+    full = jnp.zeros(dims, phase_local.dtype)
+    for mask in range(ways):
+        part = lax.dynamic_slice_in_dim(phase_local, (here ^ mask) * width, width, axis=2)
+        if mask:
+            part = lax.ppermute(part, "tile", [(d, d ^ mask) for d in range(ways)])
+        full = lax.dynamic_update_slice_in_dim(full, part, (here ^ mask) * height, axis=0)
+    arrived = full
     phase_tile = arrived.reshape(dates * later_mates, tile_pix)
     picked = jnp.take(phase_tile, slots, axis=1)
     mapping = inverse_map(couple_entry_flags)

time: 136 us -> 148 us (1.088)
  starting transfers between devices: 22.8 us -> 38.4 us
  other arithmetic: 53.6 us -> 51.5 us
  waiting for transfers between devices: 27.9 us -> 26.1 us
    ppermute x0 -> x15, starting transfers between devices: none -> 34.4 us  [local(): part = lax.ppermute(part, 'tile', [(d, d ^ mask) for d in range(ways)])]
    all_to_all x1 -> x0, starting transfers between devices: 18.8 us -> none  [local(): lax.all_to_all(phase_local, 'tile', split_axis=2, concat_axis=0, tiled=True)]
    all_to_all x1 -> x0, waiting for transfers between devices: 6.07 us -> none  [local(): lax.all_to_all(phase_local, 'tile', split_axis=2, concat_axis=0, tiled=True)]
    ppermute x0 -> x15, waiting for transfers between devices: none -> 4.59 us  [local(): part = lax.ppermute(part, 'tile', [(d, d ^ mask) for d in range(ways)])]
    unnamed x31 -> x28, local copies, waits for them, and re-layouts: 4.66 us -> 2.99 us
    another operation x0 -> x17, local copies, waits for them, and re-layouts: none -> 1.49 us
  transfers between devices with their start and end apart: 4 -> 18, of which waited for: 3 -> 4; matrix products, arithmetic and copies ran while one was open for 15% -> 14% of each run, Pallas kernels for 0% -> 0%
where the time goes in v1:
time: 148 us; the launch traced here: 147 us
  other arithmetic  51.5 us (35%)
  starting transfers between devices  38.4 us (26%)
  waiting for transfers between devices  26.1 us (18%)
  local copies, waits for them, and re-layouts  21.8 us (15%)
  between operations  5.17 us (3%)
  matrix products  4.33 us (3%)
    ppermute x15, starting transfers between devices, local(): part = lax.ppermute(part, 'tile', [(d, d ^ mask) for d in range(ways)])  34.4 us
    ppermute x3, waiting for transfers between devices, from_behind(): return lax.ppermute(block, axis, route)  21.5 us
    another operation x9, local copies, waits for them, and re-layouts, pair_stats(): jnp.stack([flat_real, flat_imag, other_energy], axis=0)  13.7 us
    add x1, other arithmetic, pair_stats(): flat_real = cross_real * cosine + cross_imag * sine  13 us
    sub x1, other arithmetic, pair_stats(): flat_imag = cross_imag * cosine - cross_real * sine  12.5 us
    reduce_sum x4, other arithmetic, looked(): jnp.sum(field.reshape(field.shape[:-2] + (rows // LOOK_ROWS, LOOK_ROWS, c...  11.3 us
    ppermute x15, waiting for transfers between devices, local(): part = lax.ppermute(part, 'tile', [(d, d ^ mask) for d in range(ways)])  4.59 us
    convert_element_type x3, other arithmetic, local(): from_behind(full_resolution_frames, 'tile', -offset)[0].astype(jnp.float32)  4.53 us
  transfers between devices with their start and end apart: 18, of which 4 were waited for; matrix products, arithmetic and copies ran while one was open for 14% of the time, Pallas kernels for 0%

profile of v1, /device:TPU:0, one launch (start us, length us, event | category | flops | bytes accessed | tf_op | source)
XLA Modules:
  0.0 147.4 jit_solution(11290325231990856544)
XLA Ops:
  19.6 1.9 %reduce_sum.37 = f32[128,512]{1,0:T(8,128)S(1)} reduce(f32[128,4,512]{2,1,0:T(4,128)} %add.287, f32[]{:T(128)} %constant.136.clone.1), dimensions={1}, to_apply=%region_1.2 | reduce | flops 196608 | bytes 1310724 | tf_op jit(solution)/shard_map/reduce_sum | solution.py:27
  22.0 1.5 %convert_element_type.39 = f32[1,2,512,512]{3,2,1,0:T(8,128)S(1)} convert(bf16[1,2,512,512]{3,2,1,0:T(8,128)(2,1)} %collective-permute-done) | non-fusion elementwise | flops 524288 | bytes 3145728 | tf_op jit(solution)/shard_map/convert_element_type | solution.py:104
  26.4 5.4 %collective-permute-done.2 = bf16[1,2,512,512]{3,2,1,0:T(8,128)(2,1)} collective-permute-done((bf16[1,2,512,512]{3,2,1,0:T(8,128)(2,1)}, bf16[1,2,512,512]{3,2,1,0:T(8,128)(2,1)}, u32[]{:S(2)}, u32[]{:S(2)}) %collective-permute-start.2) | collective-permute-done | bytes 1048608 | tf_op jit(solution)/shard_map/ppermute | solution.py:14
  31.8 1.5 %convert_element_type.41 = f32[1,2,512,512]{3,2,1,0:T(8,128)S(1)} convert(bf16[1,2,512,512]{3,2,1,0:T(8,128)(2,1)} %collective-permute-done.2) | non-fusion elementwise | flops 524288 | bytes 3145728 | tf_op jit(solution)/shard_map/convert_element_type | solution.py:104
  34.5 16.1 %collective-permute-done.1 = bf16[1,2,512,512]{3,2,1,0:T(8,128)(2,1)} collective-permute-done((bf16[1,2,512,512]{3,2,1,0:T(8,128)(2,1)}, bf16[1,2,512,512]{3,2,1,0:T(8,128)(2,1)}, u32[]{:S(2)}, u32[]{:S(2)}) %collective-permute-start.1) | collective-permute-done | bytes 1048608 | tf_op jit(solution)/shard_map/ppermute | solution.py:14
  50.6 1.5 %convert_element_type.40 = f32[1,2,512,512]{3,2,1,0:T(8,128)S(1)} convert(bf16[1,2,512,512]{3,2,1,0:T(8,128)(2,1)} %collective-permute-done.1) | non-fusion elementwise | flops 524288 | bytes 3145728 | tf_op jit(solution)/shard_map/convert_element_type | solution.py:104
  54.0 13.0 %fusion.4 = (f32[512,512]{1,0:T(8,128)}, f32[1,1,512,512]{3,2,1,0:T(8,128)S(1)}, f32[1,1,512,512]{3,2,1,0:T(8,128)S(1)}, f32[512,512]{1,0:T(8,128)}, f32[1,1,512...) fusion(f32[512,512]{1,0:T(8,128)S(1)} %copy-done.10, ...), kind=kLoop, calls=%fused_computation.19 | loop fusion | flops 7864320 | bytes 18874380 | tf_op jit(solution)/shard_map/add | solution.py:42
  67.0 12.5 %fusion.5 = (f32[512,512]{1,0:T(8,128)}, f32[512,512]{1,0:T(8,128)}, f32[512,512]{1,0:T(8,128)}) fusion(f32[1,1,512,512]{3,2,1,0:T(8,128)S(1)} %get-tuple-element.4, f32[1,1,512,512]{3,2,1,0:T(8,128)S(1)} %get-tuple-element.3, f32[512,512]{1,0:T(8,128)S(1)} %copy-done.10, f32[]{:T(128)} %bitcast.1, f32[1,1,512,512]{3,2,1,0:T(8,128)S(1)} %get-tuple-element.16, ...), kind=kLoop, calls=%fused_computation.20 | loop fusion | flops 3145728 | bytes 10485772 | tf_op jit(solution)/shard_map/sub | solution.py:43
  79.5 2.7 %stack.61 = f32[1,128,4,512]{3,2,1,0:T(4,128)} reshape(f32[512,512]{1,0:T(8,128)} %get-tuple-element.17) | data formatting | bytes 2097152 | tf_op jit(solution)/shard_map/stack | solution.py:45
  84.8 2.7 %stack.71 = f32[1,128,4,512]{3,2,1,0:T(4,128)} reshape(f32[512,512]{1,0:T(8,128)} %get-tuple-element.19) | data formatting | bytes 2097152 | tf_op jit(solution)/shard_map/stack | solution.py:45
  88.8 3.9 %maximum_reduce_fusion = f32[3,128,512]{2,1,0:T(8,128)S(1)} fusion(f32[1,128,4,512]{3,2,1,0:T(4,128)S(1)} %copy-done.6, f32[1,128,4,512]{3,2,1,0:T(4,128)} %stack.61, f32[1,128,4,512]{3,2,1,0:T(4,128)} %stack.60), kind=kLoop, calls=%fused_computation.1 | loop fusion | flops 2162688 | bytes 3932160 | tf_op jit(solution)/shard_map/reduce_sum | solution.py:27
  93.6 2.1 %maximum_reduce_fusion.2 = f32[3,128,512]{2,1,0:T(8,128)S(1)} fusion(f32[1,128,4,512]{3,2,1,0:T(4,128)S(1)} %copy-done.7, f32[1,128,4,512]{3,2,1,0:T(4,128)S(1)} %copy-done.8, f32[1,128,4,512]{3,2,1,0:T(4,128)S(1)} %copy-done.9), kind=kLoop, calls=%fused_computation.3 | loop fusion | flops 2162688 | bytes 3932160 | tf_op jit(solution)/shard_map/reduce_sum | solution.py:27
  96.9 1.5 %stack.66 = f32[1,128,4,512]{3,2,1,0:T(4,128)S(1)} reshape(f32[512,512]{1,0:T(8,128)} %get-tuple-element.18) | data formatting | bytes 2097152 | tf_op jit(solution)/shard_map/stack | solution.py:45
  99.7 3.4 %maximum_reduce_fusion.1 = f32[3,128,512]{2,1,0:T(8,128)S(1)} fusion(f32[1,128,4,512]{3,2,1,0:T(4,128)S(1)} %stack.67, f32[1,128,4,512]{3,2,1,0:T(4,128)S(1)} %stack.66, f32[1,128,4,512]{3,2,1,0:T(4,128)} %stack.65), kind=kLoop, calls=%fused_computation.2 | loop fusion | flops 2162688 | bytes 3932160 | tf_op jit(solution)/shard_map/reduce_sum | solution.py:27
  104.8 3.3 %collective-permute-start.3 = (f32[1,3,8,32]{3,2,1,0:T(8,128)S(1)}, f32[1,3,8,32]{3,2,1,0:T(8,128)S(1)}, u32[]{:S(2)}, u32[]{:S(2)}) collective-permute-start(f32[1,3,8,32]{3,2,1,0:T(8,128)S(1)} %bitcast.211), channel_id=1, source_target_pairs={{0,1},{1,0},{2,3},{3,2},{4,5},{5,4},{6,7},{7,6},{8,9},{9,8},{10,11... | collective-permute-start | bytes 9224 | tf_op jit(solution)/shard_map/ppermute | solution.py:129
  108.1 12.2 %collective-permute-start.4 = (f32[1,3,8,32]{3,2,1,0:T(8,128)S(1)}, f32[1,3,8,32]{3,2,1,0:T(8,128)S(1)}, u32[]{:S(2)}, u32[]{:S(2)}) collective-permute-start(f32[1,3,8,32]{3,2,1,0:T(8,128)S(1)} %bitcast.210), channel_id=1, source_target_pairs={{0,2},{1,3},{2,0},{3,1},{4,6},{5,7},{6,4},{7,5},{8,10},{9,11},{10,... | collective-permute-start | bytes 9224 | tf_op jit(solution)/shard_map/ppermute | solution.py:129
  120.5 1.6 %collective-permute-start.6 = (f32[1,3,8,32]{3,2,1,0:T(8,128)S(1)}, f32[1,3,8,32]{3,2,1,0:T(8,128)S(1)}, u32[]{:S(2)}, u32[]{:S(2)}) collective-permute-start(f32[1,3,8,32]{3,2,1,0:T(8,128)S(1)} %bitcast.207), channel_id=1, source_target_pairs={{0,4},{1,5},{2,6},{3,7},{4,0},{5,1},{6,2},{7,3},{8,12},{9,13},{10,... | collective-permute-start | bytes 9224 | tf_op jit(solution)/shard_map/ppermute | solution.py:129
  123.7 2.8 %collective-permute-start.8 = (f32[1,3,8,32]{3,2,1,0:T(8,128)S(1)}, f32[1,3,8,32]{3,2,1,0:T(8,128)S(1)}, u32[]{:S(2)}, u32[]{:S(2)}) collective-permute-start(f32[1,3,8,32]{3,2,1,0:T(8,128)S(1)} %bitcast.208), channel_id=1, source_target_pairs={{0,6},{1,7},{2,4},{3,5},{4,2},{5,3},{6,0},{7,1},{8,14},{9,15},{10,... | collective-permute-start | bytes 9224 | tf_op jit(solution)/shard_map/ppermute | solution.py:129
  126.7 2.4 %collective-permute-start.10 = (f32[1,3,8,32]{3,2,1,0:T(8,128)S(1)}, f32[1,3,8,32]{3,2,1,0:T(8,128)S(1)}, u32[]{:S(2)}, u32[]{:S(2)}) collective-permute-start(f32[1,3,8,32]{3,2,1,0:T(8,128)S(1)} %bitcast.204), channel_id=1, source_target_pairs={{0,8},{1,9},{2,10},{3,11},{4,12},{5,13},{6,14},{7,15},{8,0},{9,1},... | collective-permute-start | bytes 9224 | tf_op jit(solution)/shard_map/ppermute | solution.py:129
  129.2 3.7 %collective-permute-start.12 = (f32[1,3,8,32]{3,2,1,0:T(8,128)S(1)}, f32[1,3,8,32]{3,2,1,0:T(8,128)S(1)}, u32[]{:S(2)}, u32[]{:S(2)}) collective-permute-start(f32[1,3,8,32]{3,2,1,0:T(8,128)S(1)} %bitcast.202), channel_id=1, source_target_pairs={{0,10},{1,11},{2,8},{3,9},{4,14},{5,15},{6,12},{7,13},{8,2},{9,3},... | collective-permute-start | bytes 9224 | tf_op jit(solution)/shard_map/ppermute | solution.py:129
  133.1 2.4 %collective-permute-start.14 = (f32[1,3,8,32]{3,2,1,0:T(8,128)S(1)}, f32[1,3,8,32]{3,2,1,0:T(8,128)S(1)}, u32[]{:S(2)}, u32[]{:S(2)}) collective-permute-start(f32[1,3,8,32]{3,2,1,0:T(8,128)S(1)} %bitcast.200), channel_id=1, source_target_pairs={{0,12},{1,13},{2,14},{3,15},{4,8},{5,9},{6,10},{7,11},{8,4},{9,5},... | collective-permute-start | bytes 9224 | tf_op jit(solution)/shard_map/ppermute | solution.py:129
  136.4 3.4 %collective-permute-start.16 = (f32[1,3,8,32]{3,2,1,0:T(8,128)S(1)}, f32[1,3,8,32]{3,2,1,0:T(8,128)S(1)}, u32[]{:S(2)}, u32[]{:S(2)}) collective-permute-start(f32[1,3,8,32]{3,2,1,0:T(8,128)S(1)} %bitcast.198), channel_id=1, source_target_pairs={{0,14},{1,15},{2,12},{3,13},{4,10},{5,11},{6,8},{7,9},{8,6},{9,7},... | collective-permute-start | bytes 9224 | tf_op jit(solution)/shard_map/ppermute | solution.py:129
  141.1 1.6 %collective-permute-done.16 = f32[1,3,8,32]{3,2,1,0:T(8,128)S(1)} collective-permute-done((f32[1,3,8,32]{3,2,1,0:T(8,128)S(1)}, f32[1,3,8,32]{3,2,1,0:T(8,128)S(1)}, u32[]{:S(2)}, u32[]{:S(2)}) %collective-permute-start.16) | collective-permute-done | bytes 3104 | tf_op jit(solution)/shard_map/ppermute | solution.py:129
  142.8 2.9 %collective-permute-done.17 = f32[1,3,8,32]{3,2,1,0:T(8,128)S(1)} collective-permute-done((f32[1,3,8,32]{3,2,1,0:T(8,128)S(1)}, f32[1,3,8,32]{3,2,1,0:T(8,128)S(1)}, u32[]{:S(2)}, u32[]{:S(2)}) %collective-permute-start.17) | collective-permute-done | bytes 3104 | tf_op jit(solution)/shard_map/ppermute | solution.py:129
  (129 shorter events, 36.2 us)
Async XLA Ops:
  0.6 5.6 %copy-start.11 = (s32[16,3]{0,1:T(4,128)S(1)}, s32[16,3]{0,1:T(4,128)}, u32[]{:S(2)}) copy-start(s32[16,3]{0,1:T(4,128)} %param.9) | copy-start | bytes 580
  0.6 8.9 %copy-start.13 = (s32[16]{0:T(128)S(1)}, s32[16]{0:T(128)}, u32[]{:S(2)}) copy-start(s32[16]{0:T(128)} %param.11) | copy-start | bytes 196
  0.6 21.4 %collective-permute-start = (bf16[1,2,512,512]{3,2,1,0:T(8,128)(2,1)}, bf16[1,2,512,512]{3,2,1,0:T(8,128)(2,1)}, u32[]{:S(2)}, u32[]{:S(2)}) collective-permute-start(bf16[1,2,512,512]{3,2,1,0:T(8,128)(2,1)} %param.6), channel_id=1, source_target_pairs={{1,0},{2,1},{3,2},{4,3},{5,4},{6,5},{7,6},{8,7},{9,8},{10,9},{11,1... | collective-permute-start | bytes 3145736 | tf_op jit(solution)/shard_map/ppermute | solution.py:14
  2.1 29.7 %collective-permute-start.2 = (bf16[1,2,512,512]{3,2,1,0:T(8,128)(2,1)}, bf16[1,2,512,512]{3,2,1,0:T(8,128)(2,1)}, u32[]{:S(2)}, u32[]{:S(2)}) collective-permute-start(bf16[1,2,512,512]{3,2,1,0:T(8,128)(2,1)} %param.6), channel_id=1, source_target_pairs={{3,0},{4,1},{5,2},{6,3},{7,4},{8,5},{9,6},{10,7},{11,8},{12,9},{13... | collective-permute-start | bytes 3145736 | tf_op jit(solution)/shard_map/ppermute | solution.py:14
  3.4 47.3 %collective-permute-start.1 = (bf16[1,2,512,512]{3,2,1,0:T(8,128)(2,1)}, bf16[1,2,512,512]{3,2,1,0:T(8,128)(2,1)}, u32[]{:S(2)}, u32[]{:S(2)}) collective-permute-start(bf16[1,2,512,512]{3,2,1,0:T(8,128)(2,1)} %param.6), channel_id=1, source_target_pairs={{2,0},{3,1},{4,2},{5,3},{6,4},{7,5},{8,6},{9,7},{10,8},{11,9},{12,... | collective-permute-start | bytes 3145736 | tf_op jit(solution)/shard_map/ppermute | solution.py:14
  6.2 6.6 %copy-start.12 = (f32[16]{0:T(128)S(1)}, f32[16]{0:T(128)}, u32[]{:S(2)}) copy-start(f32[16]{0:T(128)} %param.8) | copy-start | bytes 196
  88.8 4.8 %copy-start.7 = (f32[1,128,4,512]{3,2,1,0:T(4,128)S(1)}, f32[1,128,4,512]{3,2,1,0:T(4,128)}, u32[]{:S(2)}) copy-start(f32[1,128,4,512]{3,2,1,0:T(4,128)} %stack.72) | copy-start | bytes 3145732
  88.8 4.8 %copy-start.8 = (f32[1,128,4,512]{3,2,1,0:T(4,128)S(1)}, f32[1,128,4,512]{3,2,1,0:T(4,128)}, u32[]{:S(2)}) copy-start(f32[1,128,4,512]{3,2,1,0:T(4,128)} %stack.71) | copy-start | bytes 3145732
  88.8 4.8 %copy-start.9 = (f32[1,128,4,512]{3,2,1,0:T(4,128)S(1)}, f32[1,128,4,512]{3,2,1,0:T(4,128)}, u32[]{:S(2)}) copy-start(f32[1,128,4,512]{3,2,1,0:T(4,128)} %stack.70) | copy-start | bytes 3145732
  104.8 19.0 %collective-permute-start.3 = (f32[1,3,8,32]{3,2,1,0:T(8,128)S(1)}, f32[1,3,8,32]{3,2,1,0:T(8,128)S(1)}, u32[]{:S(2)}, u32[]{:S(2)}) collective-permute-start(f32[1,3,8,32]{3,2,1,0:T(8,128)S(1)} %bitcast.211), channel_id=1, source_target_pairs={{0,1},{1,0},{2,3},{3,2},{4,5},{5,4},{6,7},{7,6},{8,9},{9,8},{10,11... | collective-permute-start | bytes 9224 | tf_op jit(solution)/shard_map/ppermute | solution.py:129
  108.1 18.4 %collective-permute-start.4 = (f32[1,3,8,32]{3,2,1,0:T(8,128)S(1)}, f32[1,3,8,32]{3,2,1,0:T(8,128)S(1)}, u32[]{:S(2)}, u32[]{:S(2)}) collective-permute-start(f32[1,3,8,32]{3,2,1,0:T(8,128)S(1)} %bitcast.210), channel_id=1, source_target_pairs={{0,2},{1,3},{2,0},{3,1},{4,6},{5,7},{6,4},{7,5},{8,10},{9,11},{10,... | collective-permute-start | bytes 9224 | tf_op jit(solution)/shard_map/ppermute | solution.py:129
  120.3 6.4 %collective-permute-start.5 = (f32[1,3,8,32]{3,2,1,0:T(8,128)S(1)}, f32[1,3,8,32]{3,2,1,0:T(8,128)S(1)}, u32[]{:S(2)}, u32[]{:S(2)}) collective-permute-start(f32[1,3,8,32]{3,2,1,0:T(8,128)S(1)} %bitcast.209), channel_id=1, source_target_pairs={{0,3},{1,2},{2,1},{3,0},{4,7},{5,6},{6,5},{7,4},{8,11},{9,10},{10,... | collective-permute-start | bytes 9224 | tf_op jit(solution)/shard_map/ppermute | solution.py:129
  120.5 8.6 %collective-permute-start.6 = (f32[1,3,8,32]{3,2,1,0:T(8,128)S(1)}, f32[1,3,8,32]{3,2,1,0:T(8,128)S(1)}, u32[]{:S(2)}, u32[]{:S(2)}) collective-permute-start(f32[1,3,8,32]{3,2,1,0:T(8,128)S(1)} %bitcast.207), channel_id=1, source_target_pairs={{0,4},{1,5},{2,6},{3,7},{4,0},{5,1},{6,2},{7,3},{8,12},{9,13},{10,... | collective-permute-start | bytes 9224 | tf_op jit(solution)/shard_map/ppermute | solution.py:129
  122.2 7.0 %collective-permute-start.7 = (f32[1,3,8,32]{3,2,1,0:T(8,128)S(1)}, f32[1,3,8,32]{3,2,1,0:T(8,128)S(1)}, u32[]{:S(2)}, u32[]{:S(2)}) collective-permute-start(f32[1,3,8,32]{3,2,1,0:T(8,128)S(1)} %bitcast.206), channel_id=1, source_target_pairs={{0,5},{1,4},{2,7},{3,6},{4,1},{5,0},{6,3},{7,2},{8,13},{9,12},{10,... | collective-permute-start | bytes 9224 | tf_op jit(solution)/shard_map/ppermute | solution.py:129
  123.7 9.1 %collective-permute-start.8 = (f32[1,3,8,32]{3,2,1,0:T(8,128)S(1)}, f32[1,3,8,32]{3,2,1,0:T(8,128)S(1)}, u32[]{:S(2)}, u32[]{:S(2)}) collective-permute-start(f32[1,3,8,32]{3,2,1,0:T(8,128)S(1)} %bitcast.208), channel_id=1, source_target_pairs={{0,6},{1,7},{2,4},{3,5},{4,2},{5,3},{6,0},{7,1},{8,14},{9,15},{10,... | collective-permute-start | bytes 9224 | tf_op jit(solution)/shard_map/ppermute | solution.py:129
  126.5 6.5 %collective-permute-start.9 = (f32[1,3,8,32]{3,2,1,0:T(8,128)S(1)}, f32[1,3,8,32]{3,2,1,0:T(8,128)S(1)}, u32[]{:S(2)}, u32[]{:S(2)}) collective-permute-start(f32[1,3,8,32]{3,2,1,0:T(8,128)S(1)} %bitcast.205), channel_id=1, source_target_pairs={{0,7},{1,6},{2,5},{3,4},{4,3},{5,2},{6,1},{7,0},{8,15},{9,14},{10,... | collective-permute-start | bytes 9224 | tf_op jit(solution)/shard_map/ppermute | solution.py:129
  126.7 8.7 %collective-permute-start.10 = (f32[1,3,8,32]{3,2,1,0:T(8,128)S(1)}, f32[1,3,8,32]{3,2,1,0:T(8,128)S(1)}, u32[]{:S(2)}, u32[]{:S(2)}) collective-permute-start(f32[1,3,8,32]{3,2,1,0:T(8,128)S(1)} %bitcast.204), channel_id=1, source_target_pairs={{0,8},{1,9},{2,10},{3,11},{4,12},{5,13},{6,14},{7,15},{8,0},{9,1},... | collective-permute-start | bytes 9224 | tf_op jit(solution)/shard_map/ppermute | solution.py:129
  129.2 7.2 %collective-permute-start.11 = (f32[1,3,8,32]{3,2,1,0:T(8,128)S(1)}, f32[1,3,8,32]{3,2,1,0:T(8,128)S(1)}, u32[]{:S(2)}, u32[]{:S(2)}) collective-permute-start(f32[1,3,8,32]{3,2,1,0:T(8,128)S(1)} %bitcast.203), channel_id=1, source_target_pairs={{0,9},{1,8},{2,11},{3,10},{4,13},{5,12},{6,15},{7,14},{8,1},{9,0},... | collective-permute-start | bytes 9224 | tf_op jit(solution)/shard_map/ppermute | solution.py:129
  129.2 10.6 %collective-permute-start.12 = (f32[1,3,8,32]{3,2,1,0:T(8,128)S(1)}, f32[1,3,8,32]{3,2,1,0:T(8,128)S(1)}, u32[]{:S(2)}, u32[]{:S(2)}) collective-permute-start(f32[1,3,8,32]{3,2,1,0:T(8,128)S(1)} %bitcast.202), channel_id=1, source_target_pairs={{0,10},{1,11},{2,8},{3,9},{4,14},{5,15},{6,12},{7,13},{8,2},{9,3},... | collective-permute-start | bytes 9224 | tf_op jit(solution)/shard_map/ppermute | solution.py:129
  132.9 8.2 %collective-permute-start.13 = (f32[1,3,8,32]{3,2,1,0:T(8,128)S(1)}, f32[1,3,8,32]{3,2,1,0:T(8,128)S(1)}, u32[]{:S(2)}, u32[]{:S(2)}) collective-permute-start(f32[1,3,8,32]{3,2,1,0:T(8,128)S(1)} %bitcast.201), channel_id=1, source_target_pairs={{0,11},{1,10},{2,9},{3,8},{4,15},{5,14},{6,13},{7,12},{8,3},{9,2},... | collective-permute-start | bytes 9224 | tf_op jit(solution)/shard_map/ppermute | solution.py:129
  133.1 8.0 %collective-permute-start.14 = (f32[1,3,8,32]{3,2,1,0:T(8,128)S(1)}, f32[1,3,8,32]{3,2,1,0:T(8,128)S(1)}, u32[]{:S(2)}, u32[]{:S(2)}) collective-permute-start(f32[1,3,8,32]{3,2,1,0:T(8,128)S(1)} %bitcast.200), channel_id=1, source_target_pairs={{0,12},{1,13},{2,14},{3,15},{4,8},{5,9},{6,10},{7,11},{8,4},{9,5},... | collective-permute-start | bytes 9224 | tf_op jit(solution)/shard_map/ppermute | solution.py:129
  135.5 5.6 %collective-permute-start.15 = (f32[1,3,8,32]{3,2,1,0:T(8,128)S(1)}, f32[1,3,8,32]{3,2,1,0:T(8,128)S(1)}, u32[]{:S(2)}, u32[]{:S(2)}) collective-permute-start(f32[1,3,8,32]{3,2,1,0:T(8,128)S(1)} %bitcast.199), channel_id=1, source_target_pairs={{0,13},{1,12},{2,15},{3,14},{4,9},{5,8},{6,11},{7,10},{8,5},{9,4},... | collective-permute-start | bytes 9224 | tf_op jit(solution)/shard_map/ppermute | solution.py:129
  136.4 6.4 %collective-permute-start.16 = (f32[1,3,8,32]{3,2,1,0:T(8,128)S(1)}, f32[1,3,8,32]{3,2,1,0:T(8,128)S(1)}, u32[]{:S(2)}, u32[]{:S(2)}) collective-permute-start(f32[1,3,8,32]{3,2,1,0:T(8,128)S(1)} %bitcast.198), channel_id=1, source_target_pairs={{0,14},{1,15},{2,12},{3,13},{4,10},{5,11},{6,8},{7,9},{8,6},{9,7},... | collective-permute-start | bytes 9224 | tf_op jit(solution)/shard_map/ppermute | solution.py:129
  139.8 5.9 %collective-permute-start.17 = (f32[1,3,8,32]{3,2,1,0:T(8,128)S(1)}, f32[1,3,8,32]{3,2,1,0:T(8,128)S(1)}, u32[]{:S(2)}, u32[]{:S(2)}) collective-permute-start(f32[1,3,8,32]{3,2,1,0:T(8,128)S(1)} %bitcast.197), channel_id=1, source_target_pairs={{0,15},{1,14},{2,13},{3,12},{4,11},{5,10},{6,9},{7,8},{8,7},{9,6},... | collective-permute-start | bytes 9224 | tf_op jit(solution)/shard_map/ppermute | solution.py:129
  (8 other events, 21.3 us)
